TPU v7x, 768 devices: a whole 4x8x12 slice. The times are simulated.
768 devices in a mesh: rows: 96 (over y_lo, z, core), blk: 8 (over y_hi, x).
Axes of the slice: x: 4, y: 8 (y_hi: 2, y_lo: 4; y = y_hi * 4 + y_lo), z: 12, core: 2. Of those that a mesh axis runs over, the one named last changes fastest.
Arguments:
- features: bfloat16 [196608, 256], P(('rows', 'blk')), may hold values from -32 to 32
- w_self: bfloat16 [256, 172], replicated, may hold values from -1 to 1
- w_neigh: bfloat16 [256, 172], replicated, may hold values from -0.375 to 0.375
- block_cols: int32 [1536, 6], P(('rows', 'blk')), may hold values from 0 to 15
- block_count: int32 [1536], P(('rows', 'blk')), may hold values from 1 to 6, as said below
- block_values: bfloat16 [1536, 6, 128, 128], P(('rows', 'blk')), may hold values from 0.049804688 to 1
- labels: int32 [196608], P(('rows', 'blk')), may hold values from 0 to 171
Outputs:
- loss: float32 [], replicated
- grad_self: float32 [256, 172], replicated
- grad_neigh: float32 [256, 172], replicated
- grad_features: bfloat16 [196608, 256], P(('rows', 'blk'))
Inputs may be any that keep to these rules, and one draw needn't show every extreme that they name: `block_count`: each row group's row blocks include one with exactly 6 used slots.
All inputs are finite; a program needn't handle non-finite values.
Results may differ from a plain program's by a relative error of at most 0.01.
Values may be sent and summed in bfloat16 or wider, within the bound.
No kernel may reach another device: no remote copies, remote signals or barrier semaphores. Data moves between devices by JAX's collectives and lax.ppermute only.
A program may use at most 64 MiB of HBM per device.

v0:
```python
import jax
import jax.numpy as jnp
from jax import lax
from jax.sharding import PartitionSpec as P


def per_device(features, w_self, w_neigh, block_cols, block_count, block_values, labels):
    own_rows = features.shape[0]
    nblocks = block_cols.shape[0]
    slots = block_cols.shape[1]
    width = block_values.shape[2]
    feats_n = features.shape[1]
    cycle = lax.axis_size("blk")
    nodes_all = own_rows * cycle * lax.axis_size("rows")
    used = jnp.arange(slots)[None, :] < block_count[:, None]
    live_values = jnp.where(used[:, :, None, None], block_values, jnp.zeros_like(block_values))
    degree = jnp.einsum(
        "bs,bsij->bi", used.astype(jnp.bfloat16), block_values, preferred_element_type=jnp.float32
    ).reshape(own_rows)
    group_feats = lax.all_gather(features, "blk", axis=0, tiled=True)
    row_index = block_cols[:, :, None] * width + jnp.arange(width)[None, None, :]
    picked_feats = jnp.take(group_feats, row_index.reshape(-1), axis=0).reshape(
        nblocks, slots, width, feats_n
    )
    summed = jnp.einsum(
        "bsij,bsjf->bif", live_values, picked_feats, preferred_element_type=jnp.float32
    ).reshape(own_rows, feats_n)
    aggregate = (summed / degree[:, None]).astype(jnp.bfloat16)
    logits = jnp.dot(features, w_self, preferred_element_type=jnp.float32) + jnp.dot(
        aggregate, w_neigh, preferred_element_type=jnp.float32
    )
    top = jnp.max(logits, axis=1, keepdims=True)
    shifted = jnp.exp(logits - top)
    total_exp = jnp.sum(shifted, axis=1, keepdims=True)
    lse = jnp.log(total_exp) + top
    target = jnp.arange(logits.shape[1])[None, :] == labels[:, None]
    picked = jnp.sum(jnp.where(target, logits, 0.0), axis=1)
    loss_part = jnp.sum(lse[:, 0] - picked)
    dlogits = (shifted / total_exp - target.astype(jnp.float32)).astype(jnp.bfloat16)
    factor = float(nodes_all) ** (-0.5)
    self_part = (
        lax.dot_general(
            features, dlogits, (((0,), (0,)), ((), ())), preferred_element_type=jnp.float32
        )
        * factor
    )
    neigh_part = (
        lax.dot_general(
            aggregate, dlogits, (((0,), (0,)), ((), ())), preferred_element_type=jnp.float32
        )
        * factor
    )
    loss_sum, grad_self, grad_neigh = lax.psum((loss_part, self_part, neigh_part), ("rows", "blk"))
    loss = loss_sum / nodes_all
    scaled = (
        jnp.dot(dlogits, w_neigh.T, preferred_element_type=jnp.float32) / degree[:, None]
    ).astype(jnp.bfloat16)
    rowgrad_blocks = scaled.reshape(nblocks, width, feats_n)
    mine = lax.axis_index("blk") * nblocks + jnp.arange(nblocks)
    cols = lax.all_gather(block_cols, "blk", axis=0, tiled=True)
    counts = lax.all_gather(block_count, "blk", axis=0, tiled=True)
    values = lax.all_gather(block_values, "blk", axis=0, tiled=True)
    rowgrad = lax.all_gather(rowgrad_blocks, "blk", axis=0, tiled=True)
    live = jnp.arange(slots)[None, :] < counts[:, None]
    select = ((cols[:, :, None] == mine[None, None, :]) & live[:, :, None]).astype(jnp.float32)
    terms = jnp.einsum("bsij,bif->bsjf", values, rowgrad, preferred_element_type=jnp.float32)
    partial_sum = jnp.einsum("bsc,bsjf->cjf", select, terms, precision=lax.Precision.HIGHEST)
    partial_sum = partial_sum.reshape(own_rows, feats_n)
    grad_features = (
        jnp.dot(dlogits, w_self.T, preferred_element_type=jnp.float32) + partial_sum
    ).astype(jnp.bfloat16)
    return (loss, grad_self, grad_neigh, grad_features)


def solution(mesh):
    return jax.shard_map(
        per_device,
        mesh=mesh,
        in_specs=(
            P(("rows", "blk"), None),
            P(),
            P(),
            P(("rows", "blk"), None),
            P(("rows", "blk")),
            P(("rows", "blk"), None, None, None),
            P(("rows", "blk")),
        ),
        out_specs=(P(), P(), P(), P(("rows", "blk"), None)),
        check_vma=False,
    )
```

profile of v0, /device:TPU:1, one launch (start us, length us, event | category | flops | bytes accessed | tf_op | source)
XLA Modules:
  0.0 762.0 jit_solution(11578642170995688509)
XLA Ops:
  8.0 0.7 broadcast_multiply_fusion
  8.8 1.2 convert_reduce_fusion
  10.0 0.7 fusion.24
  10.9 1.2 fusion.26
  12.1 76.7 %all-gather.5.cloned.1.call-done = bf16[2048,256]{1,0:T(8,128)(2,1)} async-done(((bf16[256,256]{1,0:T(8,128)(2,1)}), bf16[2048,256]{1,0:T(8,128)(2,1)}) %all-gather.5.cloned.1.call-update) | async-done | bytes 1048592 | tf_op jit(solution)/shard_map/all_gather | solution.py:20
  88.8 5.0 gather_fusion
  93.8 1.5 fusion.4
  95.6 0.7 fusion.12
  96.4 0.7 subtract_convert_fusion
  97.1 0.9 fusion.1
  98.8 1.3 dynamic-slice
  101.0 7.3 all-reduce
  108.3 25.1 %all-gather = s32[8,2,6]{2,1,0:T(2,128)S(1)} all-gather(s32[1,2,6]{2,1,0:T(2,128)S(1)} %bitcast.53), channel_id=1, replica_groups=mesh['rows'=96,'blk'=8] {'blk'}, dimensions={0}, use_global_device_ids=true | all-gather | bytes 432 | tf_op jit(solution)/shard_map/all_gather | solution.py:60
  134.1 128.2 %psum.21 = f32[]{:T(128)} all-reduce(f32[]{:T(128)} %subtract_reduce_fusion), channel_id=1, replica_groups=mesh['rows'=96,'blk'=8] {'rows','blk'}, use_global_device_ids=true, to_apply=%region_5.6 | all-reduce | flops 1 | bytes 8 | tf_op jit(solution)/shard_map/psum | solution.py:53
  262.9 0.9 convolution_multiply_fusion
  263.8 0.9 fusion.2
  264.7 3.9 all-gather.9.cloned.1.call-done
  268.6 8.6 %convolution_bitcast_fusion = f32[16,6,128,256]{2,3,1,0:T(8,128)} fusion(bf16[16,6,128,128]{3,2,1,0:T(8,128)(2,1)} %all-gather.9.cloned.1.call-done, bf16[16,128,256]{2,1,0:T(8,128)(2,1)} %all-gather.7.cloned.1.call-done), kind=kOutput, calls=%fused_computation.1 | convolution fusion | flops 805306368 | bytes 16777216 | tf_op jit(solution)/shard_map/bsij,bif->bsjf/dot_general | solution.py:66
  277.2 12.8 %copy.17 = f32[16,6,128,256]{3,0,1,2:T(8,128)} copy(f32[16,6,128,256]{2,3,1,0:T(8,128)} %convolution_bitcast_fusion) | data formatting | bytes 25165824 | tf_op jit(solution)/shard_map/bsij,bif->bsjf/dot_general | solution.py:66
  290.0 7.8 %convolution_bitcast_fusion.1 = f32[2,128,256]{2,0,1:T(2,128)S(1)} fusion(f32[16,6,128,256]{3,0,1,2:T(8,128)} %copy.17, pred[16,6]{0,1:T(8,128)(4,1)S(1)} %iota_compare_fusion.1, s32[16,6]{0,1:T(8,128)S(1)} %copy.15, s32[2]{0:T(128)S(1)} %iota_add_fusion.1), kind=kOutput, calls=%fused_computation.2 | convolution fusion | flops 75497856 | bytes 12845544 | tf_op jit(solution)/shard_map/bsc,bsjf->cjf/dot_general | solution.py:67
  297.9 0.9 fusion
  298.7 452.4 %all-reduce.4.cloned.1.call-done = (f32[256,172]{0,1:T(8,128)}, f32[256,172]{0,1:T(8,128)}) async-done(((f32[256,172]{0,1:T(8,128)}, f32[256,172]{0,1:T(8,128)}), (f32[256,172]{0,1:T(8,128)}, f32[256,172]{0,1:T(8,128)})) %all-reduce.4.cloned.1.call-update) | async-done | bytes 352272 | tf_op jit(solution)/shard_map/psum | solution.py:53
  751.2 1.6 copy.31
  752.8 1.6 copy.32
  (34 shorter events, 3.2 us)
Async XLA Ops:
  7.2 88.2 %copy-start = (bf16[256,172]{0,1:T(8,128)(2,1)S(1)}, bf16[256,172]{0,1:T(8,128)(2,1)}, u32[]{:S(2)}) copy-start(bf16[256,172]{0,1:T(8,128)(2,1)} %param.9) | copy-start | bytes 264196
  7.2 256.6 %copy-start.1 = (bf16[256,256]{1,0:T(8,128)(2,1)S(1)}, bf16[256,256]{1,0:T(8,128)(2,1)}, u32[]{:S(2)}) copy-start(bf16[256,256]{1,0:T(8,128)(2,1)} %param.7) | copy-start | bytes 393220
  7.2 101.1 %copy-start.3 = (s32[2,6]{1,0:T(2,128)S(1)}, s32[2,6]{1,0:T(2,128)}, u32[]{:S(2)}) copy-start(s32[2,6]{1,0:T(2,128)} %param.10) | copy-start | bytes 148
  7.2 93.6 %copy-start.4 = (s32[2]{0:T(128)S(1)}, s32[2]{0:T(128)}, u32[]{:S(2)}) copy-start(s32[2]{0:T(128)} %param.11) | copy-start | bytes 28
  7.2 81.6 %all-gather.5.cloned.1.call-start = ((), (), s32[]{:S(2)}) async-start(), calls=%async_computation | async-start | bytes 1179648 | tf_op jit(solution)/shard_map/all_gather | solution.py:20
  7.9 256.7 %all-gather.7.cloned.1.call-start = ((), (), s32[]{:S(2)}) async-start(), calls=%async_computation.1 | async-start | bytes 1179648 | tf_op jit(solution)/shard_map/all_gather | solution.py:63
  98.0 170.6 %all-gather.9.cloned.1.call-start = ((), (), s32[]{:S(2)}) async-start(), calls=%async_computation.2 | async-start | bytes 3538944 | tf_op jit(solution)/shard_map/all_gather | solution.py:62
  98.8 652.4 %all-reduce.4.cloned.1.call-start = ((), (), s32[]{:S(2)}) async-start(), calls=%async_computation.3 | async-start | bytes 720896 | tf_op jit(solution)/shard_map/psum | solution.py:53
  290.0 7.8 %copy-start.2 = (bf16[256,172]{0,1:T(8,128)(2,1)S(1)}, bf16[256,172]{0,1:T(8,128)(2,1)}, u32[]{:S(2)}) copy-start(bf16[256,172]{0,1:T(8,128)(2,1)} %param.8) | copy-start | bytes 264196
Sparse Core Ops, SparseCore 0:
  11.8 76.8 all-gather.4
  98.2 69.1 all-gather.6
  171.1 97.4 all-gather.8
  274.7 476.4 all-reduce.3
where the time goes:
time: 764 us; the launch traced here: 762 us
  waiting for transfers between devices  534 us (70%)
  blocking collectives  161 us (21%)
  matrix products  22.9 us (3%)
  local copies, waits for them, and re-layouts  22.7 us (3%)
  between operations  16.3 us (2%)
    psum x1, waiting for transfers between devices, per_device(): lax.psum((loss_part, self_part, neigh_part), ('rows', 'blk'))  452 us
    psum x1, blocking collectives, per_device(): lax.psum((loss_part, self_part, neigh_part), ('rows', 'blk'))  128 us
    all_gather x1, waiting for transfers between devices, per_device(): group_feats = lax.all_gather(features, 'blk', axis=0, tiled=True)  76.7 us
    all_gather x1, blocking collectives, per_device(): cols = lax.all_gather(block_cols, 'blk', axis=0, tiled=True)  25.1 us
  transfers between devices with their start and end apart: 4, of which 3 were waited for; matrix products, arithmetic and copies ran while one was open for 5% of the time, Pallas kernels for 0%

commit v1 on v0

v1 whole, which is shorter than its diff:
```python
import functools

import jax
import jax.numpy as jnp
from jax import lax
from jax.experimental import pallas as pl
from jax.experimental.pallas import tpu as pltpu
from jax.sharding import Mesh, PartitionSpec as P

AXES = ("y_lo", "z", "core", "y_hi", "x")
SIZES = (4, 12, 2, 2, 4)
NEAR = ("y_lo", "y_hi", "x")
FAR = ("z", "core")
N_NEAR, N_FAR = 32, 24
BS = 128
F = 256
C = 172
CP = 176
PIECE = 24
LOSS_ROW = C
ANY = pl.BlockSpec(memory_space=pl.ANY)
SMEM = pl.BlockSpec(memory_space=pltpu.SMEM)
VMEM = pl.BlockSpec(memory_space=pltpu.VMEM)
PARAMS = pltpu.CompilerParams(vmem_limit_bytes=40 * 2**20)


def split_three(value):
    high = value.astype(jnp.bfloat16).astype(jnp.float32)
    rest = value - high
    mid = rest.astype(jnp.bfloat16).astype(jnp.float32)
    return high, mid, rest - mid


def put_copies(source, out, start, sems):
    rows = pl.ds(start, source.shape[0])
    copies = [pltpu.make_async_copy(source, out.at[i, rows], sems.at[i]) for i in range(out.shape[0])]
    for copy in copies:
        copy.start()
    for copy in copies:
        copy.wait()


def copies_kernel(source, out, sems):
    put_copies(source, out, 0, sems)


def layer_kernel(
    table, feats_all, feats, w_self_t, w_neigh_t, w_self, values, labels,
    grads, keep, send, own, terms,
):
    nblocks, slots = values.shape[0], values.shape[1]
    cols = [[table[b * slots + s] for s in range(slots)] for b in range(nblocks)]
    counts = [table[nblocks * slots + b] for b in range(nblocks)]
    my_half, my_x = table[nblocks * (slots + 1)], table[nblocks * (slots + 1) + 1]

    def home(col):
        return (col // 2) % 4, (col // 8) ^ my_half, col % 2

    def start_row(col):
        owner_x, _, second = home(col)
        return pl.multiple_of((owner_x * 4 + (col // 8) * 2 + second) * BS, BS)

    live = []
    degree_col, degree_row, summed = [], [], []
    for b in range(nblocks):
        row = []
        total = None
        for s in range(slots):
            used = jnp.where(s < counts[b], 1.0, 0.0).astype(jnp.float32)
            block = values[b, s] * jnp.full((BS, BS), used, jnp.float32).astype(jnp.bfloat16)
            row.append(block)
            wide = block.astype(jnp.float32)
            total = wide if total is None else total + wide
        live.append(row)
        degree = jnp.sum(total, axis=1, keepdims=True)
        degree_col.append(degree)
        degree_row.append(jnp.broadcast_to(degree, (BS, BS)).T[0:1, :])
        picked = jnp.concatenate(
            [feats_all[pl.ds(start_row(cols[b][s]), BS), :] for s in range(slots)], axis=0
        )
        summed.append(
            jnp.dot(jnp.concatenate(row, axis=1), picked, preferred_element_type=jnp.float32) / degree
        )
    aggregate = jnp.concatenate(summed, axis=0).astype(jnp.bfloat16)
    degrees = jnp.concatenate(degree_row, axis=1)
    own_feats = feats[...]
    nt = (((1,), (1,)), ((), ()))
    logits = lax.dot_general(
        w_self_t[...], own_feats, nt, preferred_element_type=jnp.float32
    ) + lax.dot_general(w_neigh_t[...], aggregate, nt, preferred_element_type=jnp.float32)
    classes = lax.broadcasted_iota(jnp.int32, logits.shape, 0)
    real = classes < C
    top = jnp.max(jnp.where(real, logits, -3.0e38), axis=0, keepdims=True)
    shifted = jnp.where(real, jnp.exp(jnp.where(real, logits - top, 0.0)), 0.0)
    total_exp = jnp.sum(shifted, axis=0, keepdims=True)
    target = classes == labels[0:1, :]
    picked_logit = jnp.sum(jnp.where(target, logits, 0.0), axis=0, keepdims=True)
    lse = jnp.log(total_exp) + top
    loss = jnp.sum(lse - picked_logit, axis=1, keepdims=True)
    dlogits = (shifted / total_exp - jnp.where(target, 1.0, 0.0)).astype(jnp.bfloat16)

    high, mid, low = split_three(loss)
    both = (own_feats, aggregate)
    rows = lax.broadcasted_iota(jnp.int32, (CP, BS), 0)
    for q in range(4):
        side = both[q // 2][:, (q % 2) * BS : (q % 2 + 1) * BS]
        part = jnp.dot(dlogits, side, preferred_element_type=jnp.float32)
        if q == 0:
            part = jnp.where(rows == LOSS_ROW, high, part)
            part = jnp.where(rows == LOSS_ROW + 1, mid, part)
            part = jnp.where(rows == LOSS_ROW + 2, low, part)
        grads[q * CP : (q + 1) * CP, :] = part.astype(jnp.bfloat16)
    pad = grads.shape[0] - 4 * CP
    grads[4 * CP :, :] = jnp.zeros((pad, BS), jnp.bfloat16)

    own[...] = jnp.dot(w_self[...], dlogits, preferred_element_type=jnp.float32)
    scaled = (dlogits.astype(jnp.float32) / degrees).astype(jnp.bfloat16)
    terms[...] = jnp.zeros_like(terms)
    for b in range(nblocks):
        mine = scaled[:, b * BS : (b + 1) * BS]
        for s in range(slots):
            term = jnp.dot(mine, live[b][s], preferred_element_type=jnp.float32)
            owner_x, across, second = home(cols[b][s])
            delta = owner_x ^ my_x
            late = delta // 2
            early = (delta % 2) ^ late
            terms[early * 8 + late * 4 + across * 2 + second] += term
    keep[...] = terms[0:8]
    send[...] = terms[8:16].astype(jnp.bfloat16)


def halve_kernel(kept, came, keep, send):
    half = kept.shape[0] // 2
    keep[...] = kept[0:half] + came[0:half].astype(jnp.float32)
    send[...] = (kept[half:] + came[half:].astype(jnp.float32)).astype(jnp.bfloat16)


def features_kernel(kept, came, own, w_neigh, out):
    for r in range(2):
        scattered = (kept[r] + came[r].astype(jnp.float32)).astype(jnp.bfloat16)
        total = own[:, r * BS : (r + 1) * BS] + jnp.dot(
            w_neigh[...], scattered, preferred_element_type=jnp.float32
        )
        out[r * BS : (r + 1) * BS, :] = total.T.astype(jnp.bfloat16)


def spread(total, loss_here, out):
    rows = lax.broadcasted_iota(jnp.int32, total.shape, 0)
    here = LOSS_ROW % PIECE
    carries = (rows >= here) & (rows < here + 3)
    loss = jnp.sum(jnp.where(carries, total, 0.0), axis=0, keepdims=True)
    high, mid, low = split_three(loss)
    fixed = jnp.where(rows == here, high, jnp.where(rows == here + 1, mid, low))
    use = carries & (jnp.full(total.shape, loss_here[0], jnp.int32) == 1)
    out[...] = jnp.broadcast_to(jnp.where(use, fixed, total).astype(jnp.bfloat16)[None], out.shape)


def piece_kernel(loss_here, pieces, after, out):
    spread(jnp.sum(pieces[...].astype(jnp.float32), axis=0), loss_here, out)


def grads_kernel(nodes_all, pieces, loss, grad_self, grad_neigh):
    factor = float(nodes_all) ** (-0.5)
    outs = (grad_self, grad_neigh)
    for q in range(4):
        part = pieces[q * CP : (q + 1) * CP, :].astype(jnp.float32)
        if q == 0:
            carried = part[LOSS_ROW - 4 : CP, :]
            rows = lax.broadcasted_iota(jnp.int32, carried.shape, 0)
            lanes = lax.broadcasted_iota(jnp.int32, carried.shape, 1)
            use = (rows >= 4) & (rows < 7) & (lanes == 0)
            loss[0, 0] = jnp.sum(jnp.where(use, carried, 0.0)) / nodes_all
        outs[q // 2][:, (q % 2) * BS : (q % 2 + 1) * BS] = part[:C] * factor


def call(kernel, outs, in_specs, out_specs=None, scratch=(), aliases=None):
    shapes = [jax.ShapeDtypeStruct(shape, dtype) for shape, dtype in outs]
    return pl.pallas_call(
        kernel,
        out_shape=shapes,
        in_specs=in_specs,
        out_specs=out_specs or [VMEM] * len(shapes),
        scratch_shapes=list(scratch),
        input_output_aliases=aliases or {},
        compiler_params=PARAMS,
    )


def exchange(rows, axes):
    return lax.all_to_all(rows, axes, 0, 0, tiled=True)


def per_device(features, w_self, w_neigh, block_cols, block_count, block_values, labels):
    bf16, f32 = jnp.bfloat16, jnp.float32
    own_rows = features.shape[0]
    nodes_all = own_rows * 768
    y_lo, y_hi, x = (lax.axis_index(a) for a in NEAR)
    place = jnp.stack([y_hi, x]).astype(jnp.int32)
    table = jnp.concatenate([block_cols.reshape(-1), block_count, place])
    loss_here = ((y_lo * 2 + y_hi) * 4 + x == LOSS_ROW // PIECE).astype(jnp.int32).reshape(1)

    swap = [(0, 1), (1, 0)]
    both = lax.all_gather(features, "y_hi", axis=0, tiled=True)
    copies_of = [((4, 2 * own_rows, F), bf16)]
    (copies,) = call(copies_kernel, copies_of, [VMEM], [ANY], [pltpu.SemaphoreType.DMA((4,))])(both)
    feats_all = exchange(copies.reshape(8 * own_rows, F), "x")
    pad = ((0, 0), (0, CP - C))
    w_self_p, w_neigh_p = jnp.pad(w_self, pad), jnp.pad(w_neigh, pad)
    grads, keep, send, own = call(
        layer_kernel,
        [
            ((N_NEAR * PIECE, BS), bf16),
            ((8, CP, BS), f32),
            ((8, CP, BS), bf16),
            ((F, own_rows), f32),
        ],
        [SMEM] + [VMEM] * 7,
        scratch=[pltpu.VMEM((16, CP, BS), f32)],
    )(
        table, feats_all, features, w_self_p.T, w_neigh_p.T, w_self_p, block_values,
        jnp.broadcast_to(labels[None], (8, own_rows)),
    )

    came = lax.ppermute(send, "x", [(i, i ^ 1) for i in range(4)])
    keep, send = call(halve_kernel, [((4, CP, BS), f32), ((4, CP, BS), bf16)], [VMEM] * 2)(keep, came)
    came = second = lax.ppermute(send, "x", [(i, 3 - i) for i in range(4)])
    keep, send = call(halve_kernel, [((2, CP, BS), f32), ((2, CP, BS), bf16)], [VMEM] * 2)(keep, came)
    came = lax.ppermute(send, "y_hi", swap)
    (grad_features,) = call(features_kernel, [((own_rows, F), bf16)], [VMEM] * 4)(keep, came, own, w_neigh_p)

    pieces = exchange(grads, NEAR).reshape(N_NEAR, PIECE, BS)
    (pieces,) = call(piece_kernel, [((N_FAR, PIECE, BS), bf16)], [SMEM, VMEM, SMEM])(loss_here, pieces, loss_here)
    pieces = exchange(pieces.reshape(N_FAR * PIECE, BS), FAR).reshape(N_FAR, PIECE, BS)
    (pieces,) = call(piece_kernel, [((N_NEAR, PIECE, BS), bf16)], [SMEM, VMEM, ANY])(loss_here, pieces, second)
    pieces = exchange(pieces.reshape(N_NEAR * PIECE, BS), NEAR)
    loss, grad_self, grad_neigh = call(
        functools.partial(grads_kernel, nodes_all),
        [((1, 1), f32), ((C, F), f32), ((C, F), f32)],
        [VMEM],
        [SMEM, VMEM, VMEM],
    )(pieces)
    return (loss.reshape(()), grad_self.T, grad_neigh.T, grad_features)


def solution(mesh):
    fine = Mesh(mesh.devices.reshape(SIZES), AXES)
    return jax.shard_map(
        per_device,
        mesh=fine,
        in_specs=(P(AXES, None), P(), P(), P(AXES, None), P(AXES), P(AXES, None, None, None), P(AXES)),
        out_specs=(P(), P(), P(), P(AXES, None)),
        check_vma=False,
    )
```

time: 764 us -> 103 us (0.13)
  waiting for transfers between devices: 534 us -> 30.1 us
  blocking collectives: 161 us -> 9.76 us
  starting transfers between devices: 0.16 us -> 51.9 us
  matrix products: 22.9 us -> 0 us
  local copies, waits for them, and re-layouts: 22.7 us -> 2.66 us
  between operations: 16.3 us -> 0.82 us
    psum x1 -> x0, waiting for transfers between devices: 452 us -> none  [per_device(): lax.psum((loss_part, self_part, neigh_part), ('rows', 'blk'))]
    psum x1 -> x0, blocking collectives: 128 us -> none  [per_device(): lax.psum((loss_part, self_part, neigh_part), ('rows', 'blk'))]
    all_gather x3 -> x0, waiting for transfers between devices: 80.7 us -> none  [the longest x1 76.7 us: per_device(): group_feats = lax.all_gather(features, 'blk', axis=0, tiled=True)]
    all_to_all x0 -> x4, starting transfers between devices: none -> 39.9 us  [exchange(): return lax.all_to_all(rows, axes, 0, 0, tiled=True)]
    dot_general x10 -> x0, matrix products: 22.9 us -> none  [the longest x1 8.62 us: per_device(): jnp.einsum('bsij,bif->bsjf', values, rowgrad, preferred_element_type=jnp....]
    all_to_all x0 -> x4, waiting for transfers between devices: none -> 17.2 us  [exchange(): return lax.all_to_all(rows, axes, 0, 0, tiled=True)]
    all_gather x1, blocking collectives: 25.1 us -> 9.76 us  [per_device(): both = lax.all_gather(features, 'y_hi', axis=0, tiled=True)]
    ppermute x0 -> x3, waiting for transfers between devices: none -> 12.9 us  [the longest x1 7.16 us: per_device(): came = second = lax.ppermute(send, 'x', [(i, 3 - i) for i in range(4)])]
  transfers between devices with their start and end apart: 4 -> 7, of which waited for: 3 -> 5; matrix products, arithmetic and copies ran while one was open for 5% -> 1% of each run, Pallas kernels for 0% -> 2%
where the time goes in v1:
time: 103 us; the launch traced here: 102 us
  starting transfers between devices  51.9 us (50%)
  waiting for transfers between devices  30.1 us (29%)
  blocking collectives  9.76 us (9%)
  Pallas kernels  6.83 us (7%)
  local copies, waits for them, and re-layouts  2.66 us (3%)
    all_to_all x4, starting transfers between devices, exchange(): return lax.all_to_all(rows, axes, 0, 0, tiled=True)  39.9 us
    all_to_all x4, waiting for transfers between devices, exchange(): return lax.all_to_all(rows, axes, 0, 0, tiled=True)  17.2 us
    all_gather x1, blocking collectives, per_device(): both = lax.all_gather(features, 'y_hi', axis=0, tiled=True)  9.76 us
    ppermute x1, waiting for transfers between devices, per_device(): came = second = lax.ppermute(send, 'x', [(i, 3 - i) for i in range(4)])  7.16 us
    ppermute x1, starting transfers between devices, per_device(): came = lax.ppermute(send, 'y_hi', swap)  6.95 us
    ppermute x1, waiting for transfers between devices, per_device(): came = lax.ppermute(send, 'y_hi', swap)  5.74 us
    ppermute x1, starting transfers between devices, per_device(): came = lax.ppermute(send, 'x', [(i, i ^ 1) for i in range(4)])  3.14 us
    pallas_call x1, Pallas kernels, per_device(): call(layer_kernel, [((N_NEAR * PIECE, BS), bf16), ((8, CP, BS), f32), ((8...  2.57 us
  transfers between devices with their start and end apart: 7, of which 5 were waited for; matrix products, arithmetic and copies ran while one was open for 1% of the time, Pallas kernels for 2%

profile of v1, /device:TPU:1, one launch (start us, length us, event | category | flops | bytes accessed | tf_op | source)
XLA Modules:
  0.0 102.1 jit_solution(374748084840520967)
XLA Ops:
  0.6 9.8 %all_gather.3.source = bf16[512,256]{1,0:T(8,128)(2,1)S(1)} all-gather(bf16[256,256]{1,0:T(8,128)(2,1)} %feats.1), channel_id=1, replica_groups=mesh['y_lo'=4,'z'=12,'core'=2,'y_hi'=2,'x'=4] {'y_hi'}, dimensions={0}, use_global_device_ids=true | all-gather | bytes 393216 | tf_op jit(solution)/shard_map/all_gather | solution.py:203
  10.4 1.0 %shard_map.102 = bf16[4,512,256]{2,1,0:T(8,128)(2,1)} custom-call(bf16[512,256]{1,0:T(8,128)(2,1)S(1)} %all_gather.3.source), custom_call_target="tpu_custom_call" | custom-call | tf_op jit(solution)/shard_map/pallas_call | solution.py:205
  11.4 4.9 %all-to-all-start = ((bf16[4,512,256]{2,1,0:T(8,128)(2,1)}), bf16[4,512,256]{2,1,0:T(8,128)(2,1)S(1)}, u32[]{:S(2)}, u32[]{:S(2)}) async-start(bf16[4,512,256]{2,1,0:T(8,128)(2,1)} %shard_map.102), calls=%async_computation | async-start | bytes 2097152 | tf_op jit(solution)/shard_map/all_to_all | solution.py:190
  16.3 0.7 copy-done.6
  17.2 0.8 copy-done.3
  18.1 0.1 copy.14.w_neigh_t
  18.2 0.1 copy.13.w_self_t
  18.4 0.6 copy-done.5
  19.1 6.9 %all-to-all-done = bf16[4,512,256]{2,1,0:T(8,128)(2,1)S(1)} async-done(((bf16[4,512,256]{2,1,0:T(8,128)(2,1)}), bf16[4,512,256]{2,1,0:T(8,128)(2,1)S(1)}, u32[]{:S(2)}, u32[]{:S(2)}) %all-to-all-start) | async-done | bytes 1048608 | tf_op jit(solution)/shard_map/all_to_all | solution.py:190
  26.0 2.6 %shard_map.103 = (bf16[768,128]{1,0:T(8,128)(2,1)}, f32[8,176,128]{2,1,0:T(8,128)S(1)}, bf16[8,176,128]{2,1,0:T(8,128)(2,1)S(1)}, f32[256,256]{1,0:T(8,128)S(1)}) custom-call(s32[16]{0:T(128)S(1)} %pad_add_fusion.table, bf16[2048,256]{1,0:T(8,128)(2,1)S(1)} %bitcast.13, bf16[256,256]{1,0:T(8,128)(2,1)S(1)} %copy-done, bf16[176,256]{1,0:T(8,128)(2,1)S(1)} %copy.13.w_self_t, ...), custom_call_target="tpu_custom_call" | custom-call | tf_op jit(solution)/shard_map/pallas_call | solution.py:209
  28.6 12.5 %all-to-all-start.1 = ((bf16[32,24,128]{2,1,0:T(8,128)(2,1)}), bf16[32,24,128]{2,1,0:T(8,128)(2,1)S(1)}, u32[]{:S(2)}, u32[]{:S(2)}) async-start(bf16[32,24,128]{2,1,0:T(8,128)(2,1)} %bitcast.6), calls=%async_computation.1 | async-start | bytes 393216 | tf_op jit(solution)/shard_map/all_to_all | solution.py:190
  41.1 3.1 %collective-permute-start = (bf16[8,176,128]{2,1,0:T(8,128)(2,1)S(1)}, bf16[8,176,128]{2,1,0:T(8,128)(2,1)S(1)}, u32[]{:S(2)}, u32[]{:S(2)}) collective-permute-start(bf16[8,176,128]{2,1,0:T(8,128)(2,1)S(1)} %get-tuple-element.17), channel_id=1, source_target_pairs={{0,1},{1,0},{2,3},{3,2},{4,5},{5,4},{6,7},{7,6},{8,9},{9,8},{10,11... | collective-permute-start | bytes 1081352 | tf_op jit(solution)/shard_map/ppermute | solution.py:224
  44.3 7.0 %all-to-all-done.1.pieces = bf16[32,24,128]{2,1,0:T(8,128)(2,1)S(1)} async-done(((bf16[32,24,128]{2,1,0:T(8,128)(2,1)}), bf16[32,24,128]{2,1,0:T(8,128)(2,1)S(1)}, u32[]{:S(2)}, u32[]{:S(2)}) %all-to-all-start.1) | async-done | bytes 196640 | tf_op jit(solution)/shard_map/all_to_all | solution.py:190
  51.3 0.7 shard_map.104
  52.0 18.7 %all-to-all-start.2 = ((bf16[24,24,128]{2,1,0:T(8,128)(2,1)}), bf16[24,24,128]{2,1,0:T(8,128)(2,1)S(1)}, u32[]{:S(2)}, u32[]{:S(2)}) async-start(bf16[24,24,128]{2,1,0:T(8,128)(2,1)} %shard_map.104), calls=%async_computation.2 | async-start | bytes 294912 | tf_op jit(solution)/shard_map/all_to_all | solution.py:190
  70.7 1.9 %collective-permute-start.1 = (bf16[4,176,128]{2,1,0:T(8,128)(2,1)S(1)}, bf16[4,176,128]{2,1,0:T(8,128)(2,1)S(1)}, u32[]{:S(2)}, u32[]{:S(2)}) collective-permute-start(bf16[4,176,128]{2,1,0:T(8,128)(2,1)S(1)} %get-tuple-element.18), channel_id=1, source_target_pairs={{0,3},{1,2},{2,1},{3,0},{4,7},{5,6},{6,5},{7,4},{8,11},{9,10},{10,... | collective-permute-start | bytes 540680 | tf_op jit(solution)/shard_map/ppermute | solution.py:226
  72.7 7.2 %collective-permute-done.1.after.came = bf16[4,176,128]{2,1,0:T(8,128)(2,1)S(1)} collective-permute-done((bf16[4,176,128]{2,1,0:T(8,128)(2,1)S(1)}, bf16[4,176,128]{2,1,0:T(8,128)(2,1)S(1)}, u32[]{:S(2)}, u32[]{:S(2)}) %collective-permute-start.1) | collective-permute-done | bytes 180256 | tf_op jit(solution)/shard_map/ppermute | solution.py:226
  79.8 3.3 %all-to-all-done.2.pieces = bf16[24,24,128]{2,1,0:T(8,128)(2,1)S(1)} async-done(((bf16[24,24,128]{2,1,0:T(8,128)(2,1)}), bf16[24,24,128]{2,1,0:T(8,128)(2,1)S(1)}, u32[]{:S(2)}, u32[]{:S(2)}) %all-to-all-start.2) | async-done | bytes 147488 | tf_op jit(solution)/shard_map/all_to_all | solution.py:190
  83.1 0.7 shard_map.106
  83.8 3.9 %all-to-all-start.3 = ((bf16[32,24,128]{2,1,0:T(8,128)(2,1)}), bf16[32,24,128]{2,1,0:T(8,128)(2,1)S(1)}, u32[]{:S(2)}, u32[]{:S(2)}) async-start(bf16[32,24,128]{2,1,0:T(8,128)(2,1)} %shard_map.106), calls=%async_computation.3 | async-start | bytes 393216 | tf_op jit(solution)/shard_map/all_to_all | solution.py:190
  87.7 7.0 %collective-permute-start.2 = (bf16[2,176,128]{2,1,0:T(8,128)(2,1)S(1)}, bf16[2,176,128]{2,1,0:T(8,128)(2,1)S(1)}, u32[]{:S(2)}, u32[]{:S(2)}) collective-permute-start(bf16[2,176,128]{2,1,0:T(8,128)(2,1)S(1)} %get-tuple-element.24), channel_id=1, source_target_pairs={{0,4},{4,0},{1,5},{5,1},{2,6},{6,2},{3,7},{7,3},{8,12},{12,8},{9,1... | collective-permute-start | bytes 270344 | tf_op jit(solution)/shard_map/ppermute | solution.py:228
  94.7 5.7 %collective-permute-done.2.came = bf16[2,176,128]{2,1,0:T(8,128)(2,1)S(1)} collective-permute-done((bf16[2,176,128]{2,1,0:T(8,128)(2,1)S(1)}, bf16[2,176,128]{2,1,0:T(8,128)(2,1)S(1)}, u32[]{:S(2)}, u32[]{:S(2)}) %collective-permute-start.2) | collective-permute-done | bytes 90144 | tf_op jit(solution)/shard_map/ppermute | solution.py:228
  100.4 0.9 shard_map.109
  101.4 0.8 shard_map.107
  (22 shorter events, 0.5 us)
Async XLA Ops:
  11.4 5.6 %copy-start.2 = (bf16[256,172]{0,1:T(8,128)(2,1)S(1)}, bf16[256,172]{0,1:T(8,128)(2,1)}, u32[]{:S(2)}) copy-start(bf16[256,172]{0,1:T(8,128)(2,1)} %param.8) | copy-start | bytes 264196
  11.4 14.6 %all-to-all-start = ((bf16[4,512,256]{2,1,0:T(8,128)(2,1)}), bf16[4,512,256]{2,1,0:T(8,128)(2,1)S(1)}, u32[]{:S(2)}, u32[]{:S(2)}) async-start(bf16[4,512,256]{2,1,0:T(8,128)(2,1)} %shard_map.102), calls=%async_computation | async-start | bytes 2097152 | tf_op jit(solution)/shard_map/all_to_all | solution.py:190
  16.3 0.7 copy-start.6
  17.1 0.9 copy-start.3
  18.1 8.0 %copy-start.1 = (bf16[2,6,128,128]{3,2,1,0:T(8,128)(2,1)S(1)}, bf16[2,6,128,128]{3,2,1,0:T(8,128)(2,1)}, u32[]{:S(2)}) copy-start(bf16[2,6,128,128]{3,2,1,0:T(8,128)(2,1)} %values.1) | copy-start | bytes 1179652
  18.2 7.8 %copy-start = (bf16[256,256]{1,0:T(8,128)(2,1)S(1)}, bf16[256,256]{1,0:T(8,128)(2,1)}, u32[]{:S(2)}) copy-start(bf16[256,256]{1,0:T(8,128)(2,1)} %feats.1) | copy-start | bytes 393220
  18.4 0.7 copy-start.5
  19.0 7.0 %copy-start.4 = (s32[256]{0:T(256)S(1)}, s32[256]{0:T(256)}, u32[]{:S(2)}) copy-start(s32[256]{0:T(256)} %param.13) | copy-start | bytes 3076
  28.6 22.6 %all-to-all-start.1 = ((bf16[32,24,128]{2,1,0:T(8,128)(2,1)}), bf16[32,24,128]{2,1,0:T(8,128)(2,1)S(1)}, u32[]{:S(2)}, u32[]{:S(2)}) async-start(bf16[32,24,128]{2,1,0:T(8,128)(2,1)} %bitcast.6), calls=%async_computation.1 | async-start | bytes 393216 | tf_op jit(solution)/shard_map/all_to_all | solution.py:190
  41.1 29.5 %collective-permute-start = (bf16[8,176,128]{2,1,0:T(8,128)(2,1)S(1)}, bf16[8,176,128]{2,1,0:T(8,128)(2,1)S(1)}, u32[]{:S(2)}, u32[]{:S(2)}) collective-permute-start(bf16[8,176,128]{2,1,0:T(8,128)(2,1)S(1)} %get-tuple-element.17), channel_id=1, source_target_pairs={{0,1},{1,0},{2,3},{3,2},{4,5},{5,4},{6,7},{7,6},{8,9},{9,8},{10,11... | collective-permute-start | bytes 1081352 | tf_op jit(solution)/shard_map/ppermute | solution.py:224
  52.0 31.1 %all-to-all-start.2 = ((bf16[24,24,128]{2,1,0:T(8,128)(2,1)}), bf16[24,24,128]{2,1,0:T(8,128)(2,1)S(1)}, u32[]{:S(2)}, u32[]{:S(2)}) async-start(bf16[24,24,128]{2,1,0:T(8,128)(2,1)} %shard_map.104), calls=%async_computation.2 | async-start | bytes 294912 | tf_op jit(solution)/shard_map/all_to_all | solution.py:190
  70.7 9.1 %collective-permute-start.1 = (bf16[4,176,128]{2,1,0:T(8,128)(2,1)S(1)}, bf16[4,176,128]{2,1,0:T(8,128)(2,1)S(1)}, u32[]{:S(2)}, u32[]{:S(2)}) collective-permute-start(bf16[4,176,128]{2,1,0:T(8,128)(2,1)S(1)} %get-tuple-element.18), channel_id=1, source_target_pairs={{0,3},{1,2},{2,1},{3,0},{4,7},{5,6},{6,5},{7,4},{8,11},{9,10},{10,... | collective-permute-start | bytes 540680 | tf_op jit(solution)/shard_map/ppermute | solution.py:226
  83.8 17.6 %all-to-all-start.3 = ((bf16[32,24,128]{2,1,0:T(8,128)(2,1)}), bf16[32,24,128]{2,1,0:T(8,128)(2,1)S(1)}, u32[]{:S(2)}, u32[]{:S(2)}) async-start(bf16[32,24,128]{2,1,0:T(8,128)(2,1)} %shard_map.106), calls=%async_computation.3 | async-start | bytes 393216 | tf_op jit(solution)/shard_map/all_to_all | solution.py:190
  87.7 12.7 %collective-permute-start.2 = (bf16[2,176,128]{2,1,0:T(8,128)(2,1)S(1)}, bf16[2,176,128]{2,1,0:T(8,128)(2,1)S(1)}, u32[]{:S(2)}, u32[]{:S(2)}) collective-permute-start(bf16[2,176,128]{2,1,0:T(8,128)(2,1)S(1)} %get-tuple-element.24), channel_id=1, source_target_pairs={{0,4},{4,0},{1,5},{5,1},{2,6},{6,2},{3,7},{7,3},{8,12},{12,8},{9,1... | collective-permute-start | bytes 270344 | tf_op jit(solution)/shard_map/ppermute | solution.py:228

commit v2 on v1

--- a/solution.py
+++ b/solution.py
@@ -102,9 +102,9 @@
     high, mid, low = split_three(loss)
     both = (own_feats, aggregate)
     rows = lax.broadcasted_iota(jnp.int32, (CP, BS), 0)
+    wide = [jnp.dot(dlogits, side, preferred_element_type=jnp.float32) for side in both]
     for q in range(4):
-        side = both[q // 2][:, (q % 2) * BS : (q % 2 + 1) * BS]
-        part = jnp.dot(dlogits, side, preferred_element_type=jnp.float32)
+        part = wide[q // 2][:, (q % 2) * BS : (q % 2 + 1) * BS]
         if q == 0:
             part = jnp.where(rows == LOSS_ROW, high, part)
             part = jnp.where(rows == LOSS_ROW + 1, mid, part)
@@ -118,8 +118,12 @@
     terms[...] = jnp.zeros_like(terms)
     for b in range(nblocks):
         mine = scaled[:, b * BS : (b + 1) * BS]
-        for s in range(slots):
-            term = jnp.dot(mine, live[b][s], preferred_element_type=jnp.float32)
+        terms_of = []
+        for s in range(0, slots, 2):
+            pair = jnp.concatenate(live[b][s : s + 2], axis=1)
+            both_terms = jnp.dot(mine, pair, preferred_element_type=jnp.float32)
+            terms_of += [both_terms[:, :BS], both_terms[:, BS:]]
+        for s, term in enumerate(terms_of):
             owner_x, across, second = home(cols[b][s])
             delta = owner_x ^ my_x
             late = delta // 2
@@ -133,15 +137,6 @@
     half = kept.shape[0] // 2
     keep[...] = kept[0:half] + came[0:half].astype(jnp.float32)
     send[...] = (kept[half:] + came[half:].astype(jnp.float32)).astype(jnp.bfloat16)
-
-
-def features_kernel(kept, came, own, w_neigh, out):
-    for r in range(2):
-        scattered = (kept[r] + came[r].astype(jnp.float32)).astype(jnp.bfloat16)
-        total = own[:, r * BS : (r + 1) * BS] + jnp.dot(
-            w_neigh[...], scattered, preferred_element_type=jnp.float32
-        )
-        out[r * BS : (r + 1) * BS, :] = total.T.astype(jnp.bfloat16)
 
 
 def spread(total, loss_here, out):
@@ -159,7 +154,13 @@
     spread(jnp.sum(pieces[...].astype(jnp.float32), axis=0), loss_here, out)
 
 
-def grads_kernel(nodes_all, pieces, loss, grad_self, grad_neigh):
+def results_kernel(nodes_all, pieces, kept, came, own, w_neigh, loss, grad_self, grad_neigh, grad_features):
+    for r in range(2):
+        scattered = (kept[r] + came[r].astype(jnp.float32)).astype(jnp.bfloat16)
+        total = own[:, r * BS : (r + 1) * BS] + jnp.dot(
+            w_neigh[...], scattered, preferred_element_type=jnp.float32
+        )
+        grad_features[r * BS : (r + 1) * BS, :] = total.T.astype(jnp.bfloat16)
     factor = float(nodes_all) ** (-0.5)
     outs = (grad_self, grad_neigh)
     for q in range(4):
@@ -226,19 +227,17 @@
     came = second = lax.ppermute(send, "x", [(i, 3 - i) for i in range(4)])
     keep, send = call(halve_kernel, [((2, CP, BS), f32), ((2, CP, BS), bf16)], [VMEM] * 2)(keep, came)
     came = lax.ppermute(send, "y_hi", swap)
-    (grad_features,) = call(features_kernel, [((own_rows, F), bf16)], [VMEM] * 4)(keep, came, own, w_neigh_p)
-
     pieces = exchange(grads, NEAR).reshape(N_NEAR, PIECE, BS)
     (pieces,) = call(piece_kernel, [((N_FAR, PIECE, BS), bf16)], [SMEM, VMEM, SMEM])(loss_here, pieces, loss_here)
     pieces = exchange(pieces.reshape(N_FAR * PIECE, BS), FAR).reshape(N_FAR, PIECE, BS)
     (pieces,) = call(piece_kernel, [((N_NEAR, PIECE, BS), bf16)], [SMEM, VMEM, ANY])(loss_here, pieces, second)
     pieces = exchange(pieces.reshape(N_NEAR * PIECE, BS), NEAR)
-    loss, grad_self, grad_neigh = call(
-        functools.partial(grads_kernel, nodes_all),
-        [((1, 1), f32), ((C, F), f32), ((C, F), f32)],
-        [VMEM],
-        [SMEM, VMEM, VMEM],
-    )(pieces)
+    loss, grad_self, grad_neigh, grad_features = call(
+        functools.partial(results_kernel, nodes_all),
+        [((1, 1), f32), ((C, F), f32), ((C, F), f32), ((own_rows, F), bf16)],
+        [VMEM] * 5,
+        [SMEM, VMEM, VMEM, VMEM],
+    )(pieces, keep, came, own, w_neigh_p)
     return (loss.reshape(()), grad_self.T, grad_neigh.T, grad_features)
 
 

time: 103 us -> 102 us (level)
  transfers between devices with their start and end apart: 7 -> 7, of which waited for: 5 -> 5; matrix products, arithmetic and copies ran while one was open for 1% -> 1% of each run, Pallas kernels for 2% -> 1%
where the time goes in v2:
time: 102 us; the launch traced here: 101 us
  starting transfers between devices  51.9 us (51%)
  waiting for transfers between devices  30.1 us (30%)
  blocking collectives  9.76 us (10%)
  Pallas kernels  5.89 us (6%)
  local copies, waits for them, and re-layouts  2.66 us (3%)
    all_to_all x4, starting transfers between devices, exchange(): return lax.all_to_all(rows, axes, 0, 0, tiled=True)  39.9 us
    all_to_all x4, waiting for transfers between devices, exchange(): return lax.all_to_all(rows, axes, 0, 0, tiled=True)  17.2 us
    all_gather x1, blocking collectives, per_device(): both = lax.all_gather(features, 'y_hi', axis=0, tiled=True)  9.76 us
    ppermute x1, waiting for transfers between devices, per_device(): came = second = lax.ppermute(send, 'x', [(i, 3 - i) for i in range(4)])  7.16 us
    ppermute x1, starting transfers between devices, per_device(): came = lax.ppermute(send, 'y_hi', swap)  6.95 us
    ppermute x1, waiting for transfers between devices, per_device(): came = lax.ppermute(send, 'y_hi', swap)  5.74 us
    ppermute x1, starting transfers between devices, per_device(): came = lax.ppermute(send, 'x', [(i, i ^ 1) for i in range(4)])  3.14 us
    unnamed x16, local copies, waits for them, and re-layouts  2.33 us
  transfers between devices with their start and end apart: 7, of which 5 were waited for; matrix products, arithmetic and copies ran while one was open for 1% of the time, Pallas kernels for 1%

profile of v2, /device:TPU:1, one launch (start us, length us, event | category | flops | bytes accessed | tf_op | source)
XLA Modules:
  0.0 101.2 jit_solution(8476000984292773437)
XLA Ops:
  0.6 9.8 %all_gather.3.source = bf16[512,256]{1,0:T(8,128)(2,1)S(1)} all-gather(bf16[256,256]{1,0:T(8,128)(2,1)} %feats.1), channel_id=1, replica_groups=mesh['y_lo'=4,'z'=12,'core'=2,'y_hi'=2,'x'=4] {'y_hi'}, dimensions={0}, use_global_device_ids=true | all-gather | bytes 393216 | tf_op jit(solution)/shard_map/all_gather | solution.py:204
  10.4 1.0 %shard_map.102 = bf16[4,512,256]{2,1,0:T(8,128)(2,1)} custom-call(bf16[512,256]{1,0:T(8,128)(2,1)S(1)} %all_gather.3.source), custom_call_target="tpu_custom_call" | custom-call | tf_op jit(solution)/shard_map/pallas_call | solution.py:206
  11.4 4.9 %all-to-all-start = ((bf16[4,512,256]{2,1,0:T(8,128)(2,1)}), bf16[4,512,256]{2,1,0:T(8,128)(2,1)S(1)}, u32[]{:S(2)}, u32[]{:S(2)}) async-start(bf16[4,512,256]{2,1,0:T(8,128)(2,1)} %shard_map.102), calls=%async_computation | async-start | bytes 2097152 | tf_op jit(solution)/shard_map/all_to_all | solution.py:191
  16.3 0.7 copy-done.6
  17.1 0.1 copy.11
  17.2 0.8 copy-done.3
  18.1 0.1 copy.14.w_neigh_t
  18.2 0.1 copy.13.w_self_t
  18.4 0.6 copy-done.5
  19.1 6.9 %all-to-all-done = bf16[4,512,256]{2,1,0:T(8,128)(2,1)S(1)} async-done(((bf16[4,512,256]{2,1,0:T(8,128)(2,1)}), bf16[4,512,256]{2,1,0:T(8,128)(2,1)S(1)}, u32[]{:S(2)}, u32[]{:S(2)}) %all-to-all-start) | async-done | bytes 1048608 | tf_op jit(solution)/shard_map/all_to_all | solution.py:191
  26.0 2.3 %shard_map.103 = (bf16[768,128]{1,0:T(8,128)(2,1)}, f32[8,176,128]{2,1,0:T(8,128)S(1)}, bf16[8,176,128]{2,1,0:T(8,128)(2,1)S(1)}, f32[256,256]{1,0:T(8,128)S(1)}) custom-call(s32[16]{0:T(128)S(1)} %pad_add_fusion.table, bf16[2048,256]{1,0:T(8,128)(2,1)S(1)} %bitcast.13, bf16[256,256]{1,0:T(8,128)(2,1)S(1)} %copy-done, bf16[176,256]{1,0:T(8,128)(2,1)S(1)} %copy.13.w_self_t, ...), custom_call_target="tpu_custom_call" | custom-call | tf_op jit(solution)/shard_map/pallas_call | solution.py:210
  28.4 12.5 %all-to-all-start.1 = ((bf16[32,24,128]{2,1,0:T(8,128)(2,1)}), bf16[32,24,128]{2,1,0:T(8,128)(2,1)S(1)}, u32[]{:S(2)}, u32[]{:S(2)}) async-start(bf16[32,24,128]{2,1,0:T(8,128)(2,1)} %bitcast.6), calls=%async_computation.1 | async-start | bytes 393216 | tf_op jit(solution)/shard_map/all_to_all | solution.py:191
  40.9 3.1 %collective-permute-start = (bf16[8,176,128]{2,1,0:T(8,128)(2,1)S(1)}, bf16[8,176,128]{2,1,0:T(8,128)(2,1)S(1)}, u32[]{:S(2)}, u32[]{:S(2)}) collective-permute-start(bf16[8,176,128]{2,1,0:T(8,128)(2,1)S(1)} %get-tuple-element.18), channel_id=1, source_target_pairs={{0,1},{1,0},{2,3},{3,2},{4,5},{5,4},{6,7},{7,6},{8,9},{9,8},{10,11... | collective-permute-start | bytes 1081352 | tf_op jit(solution)/shard_map/ppermute | solution.py:225
  44.0 7.0 %all-to-all-done.1.pieces = bf16[32,24,128]{2,1,0:T(8,128)(2,1)S(1)} async-done(((bf16[32,24,128]{2,1,0:T(8,128)(2,1)}), bf16[32,24,128]{2,1,0:T(8,128)(2,1)S(1)}, u32[]{:S(2)}, u32[]{:S(2)}) %all-to-all-start.1) | async-done | bytes 196640 | tf_op jit(solution)/shard_map/all_to_all | solution.py:191
  51.0 0.7 shard_map.104
  51.7 18.7 %all-to-all-start.2 = ((bf16[24,24,128]{2,1,0:T(8,128)(2,1)}), bf16[24,24,128]{2,1,0:T(8,128)(2,1)S(1)}, u32[]{:S(2)}, u32[]{:S(2)}) async-start(bf16[24,24,128]{2,1,0:T(8,128)(2,1)} %shard_map.104), calls=%async_computation.2 | async-start | bytes 294912 | tf_op jit(solution)/shard_map/all_to_all | solution.py:191
  70.5 1.9 %collective-permute-start.1 = (bf16[4,176,128]{2,1,0:T(8,128)(2,1)S(1)}, bf16[4,176,128]{2,1,0:T(8,128)(2,1)S(1)}, u32[]{:S(2)}, u32[]{:S(2)}) collective-permute-start(bf16[4,176,128]{2,1,0:T(8,128)(2,1)S(1)} %get-tuple-element.19), channel_id=1, source_target_pairs={{0,3},{1,2},{2,1},{3,0},{4,7},{5,6},{6,5},{7,4},{8,11},{9,10},{10,... | collective-permute-start | bytes 540680 | tf_op jit(solution)/shard_map/ppermute | solution.py:227
  72.4 7.2 %collective-permute-done.1.after.came = bf16[4,176,128]{2,1,0:T(8,128)(2,1)S(1)} collective-permute-done((bf16[4,176,128]{2,1,0:T(8,128)(2,1)S(1)}, bf16[4,176,128]{2,1,0:T(8,128)(2,1)S(1)}, u32[]{:S(2)}, u32[]{:S(2)}) %collective-permute-start.1) | collective-permute-done | bytes 180256 | tf_op jit(solution)/shard_map/ppermute | solution.py:227
  79.6 3.3 %all-to-all-done.2.pieces = bf16[24,24,128]{2,1,0:T(8,128)(2,1)S(1)} async-done(((bf16[24,24,128]{2,1,0:T(8,128)(2,1)}), bf16[24,24,128]{2,1,0:T(8,128)(2,1)S(1)}, u32[]{:S(2)}, u32[]{:S(2)}) %all-to-all-start.2) | async-done | bytes 147488 | tf_op jit(solution)/shard_map/all_to_all | solution.py:191
  82.9 0.7 shard_map.106
  83.6 3.9 %all-to-all-start.3 = ((bf16[32,24,128]{2,1,0:T(8,128)(2,1)}), bf16[32,24,128]{2,1,0:T(8,128)(2,1)S(1)}, u32[]{:S(2)}, u32[]{:S(2)}) async-start(bf16[32,24,128]{2,1,0:T(8,128)(2,1)} %shard_map.106), calls=%async_computation.3 | async-start | bytes 393216 | tf_op jit(solution)/shard_map/all_to_all | solution.py:191
  87.5 7.0 %collective-permute-start.2 = (bf16[2,176,128]{2,1,0:T(8,128)(2,1)S(1)}, bf16[2,176,128]{2,1,0:T(8,128)(2,1)S(1)}, u32[]{:S(2)}, u32[]{:S(2)}) collective-permute-start(bf16[2,176,128]{2,1,0:T(8,128)(2,1)S(1)} %get-tuple-element.22), channel_id=1, source_target_pairs={{0,4},{4,0},{1,5},{5,1},{2,6},{6,2},{3,7},{7,3},{8,12},{12,8},{9,1... | collective-permute-start | bytes 270344 | tf_op jit(solution)/shard_map/ppermute | solution.py:229
  94.4 5.7 %collective-permute-done.2.came = bf16[2,176,128]{2,1,0:T(8,128)(2,1)S(1)} collective-permute-done((bf16[2,176,128]{2,1,0:T(8,128)(2,1)S(1)}, bf16[2,176,128]{2,1,0:T(8,128)(2,1)S(1)}, u32[]{:S(2)}, u32[]{:S(2)}) %collective-permute-start.2) | collective-permute-done | bytes 90144 | tf_op jit(solution)/shard_map/ppermute | solution.py:229
  100.2 1.0 shard_map.108
  (21 shorter events, 0.4 us)
Async XLA Ops:
  11.4 5.6 %copy-start.2 = (bf16[256,172]{0,1:T(8,128)(2,1)S(1)}, bf16[256,172]{0,1:T(8,128)(2,1)}, u32[]{:S(2)}) copy-start(bf16[256,172]{0,1:T(8,128)(2,1)} %param.8) | copy-start | bytes 264196
  11.4 14.6 %all-to-all-start = ((bf16[4,512,256]{2,1,0:T(8,128)(2,1)}), bf16[4,512,256]{2,1,0:T(8,128)(2,1)S(1)}, u32[]{:S(2)}, u32[]{:S(2)}) async-start(bf16[4,512,256]{2,1,0:T(8,128)(2,1)} %shard_map.102), calls=%async_computation | async-start | bytes 2097152 | tf_op jit(solution)/shard_map/all_to_all | solution.py:191
  16.3 0.7 copy-start.6
  17.1 0.9 copy-start.3
  18.1 8.0 %copy-start.1 = (bf16[2,6,128,128]{3,2,1,0:T(8,128)(2,1)S(1)}, bf16[2,6,128,128]{3,2,1,0:T(8,128)(2,1)}, u32[]{:S(2)}) copy-start(bf16[2,6,128,128]{3,2,1,0:T(8,128)(2,1)} %values.1) | copy-start | bytes 1179652
  18.2 7.8 %copy-start = (bf16[256,256]{1,0:T(8,128)(2,1)S(1)}, bf16[256,256]{1,0:T(8,128)(2,1)}, u32[]{:S(2)}) copy-start(bf16[256,256]{1,0:T(8,128)(2,1)} %feats.1) | copy-start | bytes 393220
  18.4 0.7 copy-start.5
  19.0 7.0 %copy-start.4 = (s32[256]{0:T(256)S(1)}, s32[256]{0:T(256)}, u32[]{:S(2)}) copy-start(s32[256]{0:T(256)} %param.13) | copy-start | bytes 3076
  28.4 22.7 %all-to-all-start.1 = ((bf16[32,24,128]{2,1,0:T(8,128)(2,1)}), bf16[32,24,128]{2,1,0:T(8,128)(2,1)S(1)}, u32[]{:S(2)}, u32[]{:S(2)}) async-start(bf16[32,24,128]{2,1,0:T(8,128)(2,1)} %bitcast.6), calls=%async_computation.1 | async-start | bytes 393216 | tf_op jit(solution)/shard_map/all_to_all | solution.py:191
  40.9 29.5 %collective-permute-start = (bf16[8,176,128]{2,1,0:T(8,128)(2,1)S(1)}, bf16[8,176,128]{2,1,0:T(8,128)(2,1)S(1)}, u32[]{:S(2)}, u32[]{:S(2)}) collective-permute-start(bf16[8,176,128]{2,1,0:T(8,128)(2,1)S(1)} %get-tuple-element.18), channel_id=1, source_target_pairs={{0,1},{1,0},{2,3},{3,2},{4,5},{5,4},{6,7},{7,6},{8,9},{9,8},{10,11... | collective-permute-start | bytes 1081352 | tf_op jit(solution)/shard_map/ppermute | solution.py:225
  51.7 31.1 %all-to-all-start.2 = ((bf16[24,24,128]{2,1,0:T(8,128)(2,1)}), bf16[24,24,128]{2,1,0:T(8,128)(2,1)S(1)}, u32[]{:S(2)}, u32[]{:S(2)}) async-start(bf16[24,24,128]{2,1,0:T(8,128)(2,1)} %shard_map.104), calls=%async_computation.2 | async-start | bytes 294912 | tf_op jit(solution)/shard_map/all_to_all | solution.py:191
  70.5 9.1 %collective-permute-start.1 = (bf16[4,176,128]{2,1,0:T(8,128)(2,1)S(1)}, bf16[4,176,128]{2,1,0:T(8,128)(2,1)S(1)}, u32[]{:S(2)}, u32[]{:S(2)}) collective-permute-start(bf16[4,176,128]{2,1,0:T(8,128)(2,1)S(1)} %get-tuple-element.19), channel_id=1, source_target_pairs={{0,3},{1,2},{2,1},{3,0},{4,7},{5,6},{6,5},{7,4},{8,11},{9,10},{10,... | collective-permute-start | bytes 540680 | tf_op jit(solution)/shard_map/ppermute | solution.py:227
  83.6 16.6 %all-to-all-start.3 = ((bf16[32,24,128]{2,1,0:T(8,128)(2,1)}), bf16[32,24,128]{2,1,0:T(8,128)(2,1)S(1)}, u32[]{:S(2)}, u32[]{:S(2)}) async-start(bf16[32,24,128]{2,1,0:T(8,128)(2,1)} %shard_map.106), calls=%async_computation.3 | async-start | bytes 393216 | tf_op jit(solution)/shard_map/all_to_all | solution.py:191
  87.5 12.7 %collective-permute-start.2 = (bf16[2,176,128]{2,1,0:T(8,128)(2,1)S(1)}, bf16[2,176,128]{2,1,0:T(8,128)(2,1)S(1)}, u32[]{:S(2)}, u32[]{:S(2)}) collective-permute-start(bf16[2,176,128]{2,1,0:T(8,128)(2,1)S(1)} %get-tuple-element.22), channel_id=1, source_target_pairs={{0,4},{4,0},{1,5},{5,1},{2,6},{6,2},{3,7},{7,3},{8,12},{12,8},{9,1... | collective-permute-start | bytes 270344 | tf_op jit(solution)/shard_map/ppermute | solution.py:229

commit v3 on v2

--- a/solution.py
+++ b/solution.py
@@ -9,7 +9,7 @@
 
 AXES = ("y_lo", "z", "core", "y_hi", "x")
 SIZES = (4, 12, 2, 2, 4)
-NEAR = ("y_lo", "y_hi", "x")
+NEAR = ("x", "y_hi", "y_lo")
 FAR = ("z", "core")
 N_NEAR, N_FAR = 32, 24
 BS = 128
@@ -195,10 +195,10 @@
     bf16, f32 = jnp.bfloat16, jnp.float32
     own_rows = features.shape[0]
     nodes_all = own_rows * 768
-    y_lo, y_hi, x = (lax.axis_index(a) for a in NEAR)
+    x, y_hi, y_lo = (lax.axis_index(a) for a in NEAR)
     place = jnp.stack([y_hi, x]).astype(jnp.int32)
     table = jnp.concatenate([block_cols.reshape(-1), block_count, place])
-    loss_here = ((y_lo * 2 + y_hi) * 4 + x == LOSS_ROW // PIECE).astype(jnp.int32).reshape(1)
+    loss_here = ((x * 2 + y_hi) * 4 + y_lo == LOSS_ROW // PIECE).astype(jnp.int32).reshape(1)
 
     swap = [(0, 1), (1, 0)]
     both = lax.all_gather(features, "y_hi", axis=0, tiled=True)

time: 102 us -> 101 us (level)
  waiting for transfers between devices: 30.1 us -> 28.4 us
where the time goes in v3:
time: 101 us; the launch traced here: 100 us
  starting transfers between devices  52.8 us (52%)
  waiting for transfers between devices  28.4 us (28%)
  blocking collectives  9.76 us (10%)
  Pallas kernels  5.89 us (6%)
  local copies, waits for them, and re-layouts  2.66 us (3%)
    all_to_all x4, starting transfers between devices, exchange(): return lax.all_to_all(rows, axes, 0, 0, tiled=True)  39.8 us
    all_to_all x4, waiting for transfers between devices, exchange(): return lax.all_to_all(rows, axes, 0, 0, tiled=True)  16.5 us
    all_gather x1, blocking collectives, per_device(): both = lax.all_gather(features, 'y_hi', axis=0, tiled=True)  9.76 us
    ppermute x1, starting transfers between devices, per_device(): came = lax.ppermute(send, 'y_hi', swap)  6.97 us
    ppermute x1, waiting for transfers between devices, per_device(): came = second = lax.ppermute(send, 'x', [(i, 3 - i) for i in range(4)])  6.25 us
    ppermute x1, waiting for transfers between devices, per_device(): came = lax.ppermute(send, 'y_hi', swap)  5.63 us
    ppermute x1, starting transfers between devices, per_device(): came = lax.ppermute(send, 'x', [(i, i ^ 1) for i in range(4)])  3.14 us
    ppermute x1, starting transfers between devices, per_device(): came = second = lax.ppermute(send, 'x', [(i, 3 - i) for i in range(4)])  2.83 us
  transfers between devices with their start and end apart: 7, of which 5 were waited for; matrix products, arithmetic and copies ran while one was open for 1% of the time, Pallas kernels for 1%

profile of v3, /device:TPU:1, one launch (start us, length us, event | category | flops | bytes accessed | tf_op | source)
XLA Modules:
  0.0 100.4 jit_solution(1343377804596658419)
XLA Ops:
  0.6 9.8 %all_gather.3.source = bf16[512,256]{1,0:T(8,128)(2,1)S(1)} all-gather(bf16[256,256]{1,0:T(8,128)(2,1)} %feats.1), channel_id=1, replica_groups=mesh['y_lo'=4,'z'=12,'core'=2,'y_hi'=2,'x'=4] {'y_hi'}, dimensions={0}, use_global_device_ids=true | all-gather | bytes 393216 | tf_op jit(solution)/shard_map/all_gather | solution.py:204
  10.4 1.0 %shard_map.102 = bf16[4,512,256]{2,1,0:T(8,128)(2,1)} custom-call(bf16[512,256]{1,0:T(8,128)(2,1)S(1)} %all_gather.3.source), custom_call_target="tpu_custom_call" | custom-call | tf_op jit(solution)/shard_map/pallas_call | solution.py:206
  11.4 4.9 %all-to-all-start = ((bf16[4,512,256]{2,1,0:T(8,128)(2,1)}), bf16[4,512,256]{2,1,0:T(8,128)(2,1)S(1)}, u32[]{:S(2)}, u32[]{:S(2)}) async-start(bf16[4,512,256]{2,1,0:T(8,128)(2,1)} %shard_map.102), calls=%async_computation | async-start | bytes 2097152 | tf_op jit(solution)/shard_map/all_to_all | solution.py:191
  16.3 0.7 copy-done.6
  17.1 0.1 copy.11
  17.2 0.8 copy-done.3
  18.1 0.1 copy.14.w_neigh_t
  18.2 0.1 copy.13.w_self_t
  18.4 0.6 copy-done.5
  19.1 6.9 %all-to-all-done = bf16[4,512,256]{2,1,0:T(8,128)(2,1)S(1)} async-done(((bf16[4,512,256]{2,1,0:T(8,128)(2,1)}), bf16[4,512,256]{2,1,0:T(8,128)(2,1)S(1)}, u32[]{:S(2)}, u32[]{:S(2)}) %all-to-all-start) | async-done | bytes 1048608 | tf_op jit(solution)/shard_map/all_to_all | solution.py:191
  26.0 2.3 %shard_map.103 = (bf16[768,128]{1,0:T(8,128)(2,1)}, f32[8,176,128]{2,1,0:T(8,128)S(1)}, bf16[8,176,128]{2,1,0:T(8,128)(2,1)S(1)}, f32[256,256]{1,0:T(8,128)S(1)}) custom-call(s32[16]{0:T(128)S(1)} %pad_add_fusion.table, bf16[2048,256]{1,0:T(8,128)(2,1)S(1)} %bitcast.13, bf16[256,256]{1,0:T(8,128)(2,1)S(1)} %copy-done, bf16[176,256]{1,0:T(8,128)(2,1)S(1)} %copy.13.w_self_t, ...), custom_call_target="tpu_custom_call" | custom-call | tf_op jit(solution)/shard_map/pallas_call | solution.py:210
  28.4 12.5 %all-to-all-start.1 = ((bf16[32,24,128]{2,1,0:T(8,128)(2,1)}), bf16[32,24,128]{2,1,0:T(8,128)(2,1)S(1)}, u32[]{:S(2)}, u32[]{:S(2)}) async-start(bf16[32,24,128]{2,1,0:T(8,128)(2,1)} %bitcast.6), calls=%async_computation.1 | async-start | bytes 393216 | tf_op jit(solution)/shard_map/all_to_all | solution.py:191
  40.9 3.1 %collective-permute-start = (bf16[8,176,128]{2,1,0:T(8,128)(2,1)S(1)}, bf16[8,176,128]{2,1,0:T(8,128)(2,1)S(1)}, u32[]{:S(2)}, u32[]{:S(2)}) collective-permute-start(bf16[8,176,128]{2,1,0:T(8,128)(2,1)S(1)} %get-tuple-element.18), channel_id=1, source_target_pairs={{0,1},{1,0},{2,3},{3,2},{4,5},{5,4},{6,7},{7,6},{8,9},{9,8},{10,11... | collective-permute-start | bytes 1081352 | tf_op jit(solution)/shard_map/ppermute | solution.py:225
  44.0 6.3 %all-to-all-done.1.pieces = bf16[32,24,128]{2,1,0:T(8,128)(2,1)S(1)} async-done(((bf16[32,24,128]{2,1,0:T(8,128)(2,1)}), bf16[32,24,128]{2,1,0:T(8,128)(2,1)S(1)}, u32[]{:S(2)}, u32[]{:S(2)}) %all-to-all-start.1) | async-done | bytes 196640 | tf_op jit(solution)/shard_map/all_to_all | solution.py:191
  50.3 0.7 shard_map.104
  51.0 18.6 %all-to-all-start.2 = ((bf16[24,24,128]{2,1,0:T(8,128)(2,1)}), bf16[24,24,128]{2,1,0:T(8,128)(2,1)S(1)}, u32[]{:S(2)}, u32[]{:S(2)}) async-start(bf16[24,24,128]{2,1,0:T(8,128)(2,1)} %shard_map.104), calls=%async_computation.2 | async-start | bytes 294912 | tf_op jit(solution)/shard_map/all_to_all | solution.py:191
  69.7 2.8 %collective-permute-start.1 = (bf16[4,176,128]{2,1,0:T(8,128)(2,1)S(1)}, bf16[4,176,128]{2,1,0:T(8,128)(2,1)S(1)}, u32[]{:S(2)}, u32[]{:S(2)}) collective-permute-start(bf16[4,176,128]{2,1,0:T(8,128)(2,1)S(1)} %get-tuple-element.19), channel_id=1, source_target_pairs={{0,3},{1,2},{2,1},{3,0},{4,7},{5,6},{6,5},{7,4},{8,11},{9,10},{10,... | collective-permute-start | bytes 540680 | tf_op jit(solution)/shard_map/ppermute | solution.py:227
  72.6 6.2 %collective-permute-done.1.after.came = bf16[4,176,128]{2,1,0:T(8,128)(2,1)S(1)} collective-permute-done((bf16[4,176,128]{2,1,0:T(8,128)(2,1)S(1)}, bf16[4,176,128]{2,1,0:T(8,128)(2,1)S(1)}, u32[]{:S(2)}, u32[]{:S(2)}) %collective-permute-start.1) | collective-permute-done | bytes 180256 | tf_op jit(solution)/shard_map/ppermute | solution.py:227
  78.8 3.3 %all-to-all-done.2.pieces = bf16[24,24,128]{2,1,0:T(8,128)(2,1)S(1)} async-done(((bf16[24,24,128]{2,1,0:T(8,128)(2,1)}), bf16[24,24,128]{2,1,0:T(8,128)(2,1)S(1)}, u32[]{:S(2)}, u32[]{:S(2)}) %all-to-all-start.2) | async-done | bytes 147488 | tf_op jit(solution)/shard_map/all_to_all | solution.py:191
  82.1 0.7 shard_map.106
  82.8 3.9 %all-to-all-start.3 = ((bf16[32,24,128]{2,1,0:T(8,128)(2,1)}), bf16[32,24,128]{2,1,0:T(8,128)(2,1)S(1)}, u32[]{:S(2)}, u32[]{:S(2)}) async-start(bf16[32,24,128]{2,1,0:T(8,128)(2,1)} %shard_map.106), calls=%async_computation.3 | async-start | bytes 393216 | tf_op jit(solution)/shard_map/all_to_all | solution.py:191
  86.7 7.0 %collective-permute-start.2 = (bf16[2,176,128]{2,1,0:T(8,128)(2,1)S(1)}, bf16[2,176,128]{2,1,0:T(8,128)(2,1)S(1)}, u32[]{:S(2)}, u32[]{:S(2)}) collective-permute-start(bf16[2,176,128]{2,1,0:T(8,128)(2,1)S(1)} %get-tuple-element.22), channel_id=1, source_target_pairs={{0,4},{4,0},{1,5},{5,1},{2,6},{6,2},{3,7},{7,3},{8,12},{12,8},{9,1... | collective-permute-start | bytes 270344 | tf_op jit(solution)/shard_map/ppermute | solution.py:229
  93.7 5.6 %collective-permute-done.2.came = bf16[2,176,128]{2,1,0:T(8,128)(2,1)S(1)} collective-permute-done((bf16[2,176,128]{2,1,0:T(8,128)(2,1)S(1)}, bf16[2,176,128]{2,1,0:T(8,128)(2,1)S(1)}, u32[]{:S(2)}, u32[]{:S(2)}) %collective-permute-start.2) | collective-permute-done | bytes 90144 | tf_op jit(solution)/shard_map/ppermute | solution.py:229
  99.3 1.0 %shard_map.108 = (f32[1,1]{1,0:T(1,128)}, f32[172,256]{1,0:T(8,128)}, f32[172,256]{1,0:T(8,128)}, bf16[256,256]{1,0:T(8,128)(2,1)}) custom-call(bf16[768,128]{1,0:T(8,128)(2,1)S(1)} %bitcast.14, f32[2,176,128]{2,1,0:T(8,128)S(1)} %get-tuple-element.21.kept, bf16[2,176,128]{2,1,0:T(8,128)(2,1)S(1)} %collective-permute-done.2.came, ...), custom_call_target="tpu_custom_call" | custom-call | tf_op jit(solution)/shard_map/pallas_call | solution.py:235
  (21 shorter events, 0.4 us)
Async XLA Ops:
  11.4 5.6 %copy-start.2 = (bf16[256,172]{0,1:T(8,128)(2,1)S(1)}, bf16[256,172]{0,1:T(8,128)(2,1)}, u32[]{:S(2)}) copy-start(bf16[256,172]{0,1:T(8,128)(2,1)} %param.8) | copy-start | bytes 264196
  11.4 14.6 %all-to-all-start = ((bf16[4,512,256]{2,1,0:T(8,128)(2,1)}), bf16[4,512,256]{2,1,0:T(8,128)(2,1)S(1)}, u32[]{:S(2)}, u32[]{:S(2)}) async-start(bf16[4,512,256]{2,1,0:T(8,128)(2,1)} %shard_map.102), calls=%async_computation | async-start | bytes 2097152 | tf_op jit(solution)/shard_map/all_to_all | solution.py:191
  16.3 0.7 copy-start.6
  17.1 0.9 copy-start.3
  18.1 8.0 %copy-start.1 = (bf16[2,6,128,128]{3,2,1,0:T(8,128)(2,1)S(1)}, bf16[2,6,128,128]{3,2,1,0:T(8,128)(2,1)}, u32[]{:S(2)}) copy-start(bf16[2,6,128,128]{3,2,1,0:T(8,128)(2,1)} %values.1) | copy-start | bytes 1179652
  18.2 7.8 %copy-start = (bf16[256,256]{1,0:T(8,128)(2,1)S(1)}, bf16[256,256]{1,0:T(8,128)(2,1)}, u32[]{:S(2)}) copy-start(bf16[256,256]{1,0:T(8,128)(2,1)} %feats.1) | copy-start | bytes 393220
  18.4 0.7 copy-start.5
  19.0 7.0 %copy-start.4 = (s32[256]{0:T(256)S(1)}, s32[256]{0:T(256)}, u32[]{:S(2)}) copy-start(s32[256]{0:T(256)} %param.13) | copy-start | bytes 3076
  28.4 22.0 %all-to-all-start.1 = ((bf16[32,24,128]{2,1,0:T(8,128)(2,1)}), bf16[32,24,128]{2,1,0:T(8,128)(2,1)S(1)}, u32[]{:S(2)}, u32[]{:S(2)}) async-start(bf16[32,24,128]{2,1,0:T(8,128)(2,1)} %bitcast.6), calls=%async_computation.1 | async-start | bytes 393216 | tf_op jit(solution)/shard_map/all_to_all | solution.py:191
  40.9 28.8 %collective-permute-start = (bf16[8,176,128]{2,1,0:T(8,128)(2,1)S(1)}, bf16[8,176,128]{2,1,0:T(8,128)(2,1)S(1)}, u32[]{:S(2)}, u32[]{:S(2)}) collective-permute-start(bf16[8,176,128]{2,1,0:T(8,128)(2,1)S(1)} %get-tuple-element.18), channel_id=1, source_target_pairs={{0,1},{1,0},{2,3},{3,2},{4,5},{5,4},{6,7},{7,6},{8,9},{9,8},{10,11... | collective-permute-start | bytes 1081352 | tf_op jit(solution)/shard_map/ppermute | solution.py:225
  51.0 31.1 %all-to-all-start.2 = ((bf16[24,24,128]{2,1,0:T(8,128)(2,1)}), bf16[24,24,128]{2,1,0:T(8,128)(2,1)S(1)}, u32[]{:S(2)}, u32[]{:S(2)}) async-start(bf16[24,24,128]{2,1,0:T(8,128)(2,1)} %shard_map.104), calls=%async_computation.2 | async-start | bytes 294912 | tf_op jit(solution)/shard_map/all_to_all | solution.py:191
  69.7 9.1 %collective-permute-start.1 = (bf16[4,176,128]{2,1,0:T(8,128)(2,1)S(1)}, bf16[4,176,128]{2,1,0:T(8,128)(2,1)S(1)}, u32[]{:S(2)}, u32[]{:S(2)}) collective-permute-start(bf16[4,176,128]{2,1,0:T(8,128)(2,1)S(1)} %get-tuple-element.19), channel_id=1, source_target_pairs={{0,3},{1,2},{2,1},{3,0},{4,7},{5,6},{6,5},{7,4},{8,11},{9,10},{10,... | collective-permute-start | bytes 540680 | tf_op jit(solution)/shard_map/ppermute | solution.py:227
  82.8 16.5 %all-to-all-start.3 = ((bf16[32,24,128]{2,1,0:T(8,128)(2,1)}), bf16[32,24,128]{2,1,0:T(8,128)(2,1)S(1)}, u32[]{:S(2)}, u32[]{:S(2)}) async-start(bf16[32,24,128]{2,1,0:T(8,128)(2,1)} %shard_map.106), calls=%async_computation.3 | async-start | bytes 393216 | tf_op jit(solution)/shard_map/all_to_all | solution.py:191
  86.7 12.6 %collective-permute-start.2 = (bf16[2,176,128]{2,1,0:T(8,128)(2,1)S(1)}, bf16[2,176,128]{2,1,0:T(8,128)(2,1)S(1)}, u32[]{:S(2)}, u32[]{:S(2)}) collective-permute-start(bf16[2,176,128]{2,1,0:T(8,128)(2,1)S(1)} %get-tuple-element.22), channel_id=1, source_target_pairs={{0,4},{4,0},{1,5},{5,1},{2,6},{6,2},{3,7},{7,3},{8,12},{12,8},{9,1... | collective-permute-start | bytes 270344 | tf_op jit(solution)/shard_map/ppermute | solution.py:229

commit v4 on v3

--- a/solution.py
+++ b/solution.py
@@ -61,7 +61,7 @@
         return pl.multiple_of((owner_x * 4 + (col // 8) * 2 + second) * BS, BS)
 
     live = []
-    degree_col, degree_row, summed = [], [], []
+    degree_col, summed = [], []
     for b in range(nblocks):
         row = []
         total = None
@@ -74,7 +74,6 @@
         live.append(row)
         degree = jnp.sum(total, axis=1, keepdims=True)
         degree_col.append(degree)
-        degree_row.append(jnp.broadcast_to(degree, (BS, BS)).T[0:1, :])
         picked = jnp.concatenate(
             [feats_all[pl.ds(start_row(cols[b][s]), BS), :] for s in range(slots)], axis=0
         )
@@ -82,7 +81,9 @@
             jnp.dot(jnp.concatenate(row, axis=1), picked, preferred_element_type=jnp.float32) / degree
         )
     aggregate = jnp.concatenate(summed, axis=0).astype(jnp.bfloat16)
-    degrees = jnp.concatenate(degree_row, axis=1)
+    lanes = lax.broadcasted_iota(jnp.int32, (BS, BS), 1)
+    turned = jnp.where(lanes == 0, degree_col[0], degree_col[1]).T
+    degrees = jnp.concatenate([turned[0:1, :], turned[1:2, :]], axis=1)
     own_feats = feats[...]
     nt = (((1,), (1,)), ((), ()))
     logits = lax.dot_general(
@@ -91,7 +92,7 @@
     classes = lax.broadcasted_iota(jnp.int32, logits.shape, 0)
     real = classes < C
     top = jnp.max(jnp.where(real, logits, -3.0e38), axis=0, keepdims=True)
-    shifted = jnp.where(real, jnp.exp(jnp.where(real, logits - top, 0.0)), 0.0)
+    shifted = jnp.where(real, jnp.exp(logits - top), 0.0)
     total_exp = jnp.sum(shifted, axis=0, keepdims=True)
     target = classes == labels[0:1, :]
     picked_logit = jnp.sum(jnp.where(target, logits, 0.0), axis=0, keepdims=True)

time: 101 us -> 101 us (level)
  no operation moved by 1% of the time
where the time goes in v4:
time: 101 us; the launch traced here: 100 us
  starting transfers between devices  52.8 us (52%)
  waiting for transfers between devices  28.4 us (28%)
  blocking collectives  9.76 us (10%)
  Pallas kernels  5.89 us (6%)
  local copies, waits for them, and re-layouts  2.66 us (3%)
    all_to_all x4, starting transfers between devices, exchange(): return lax.all_to_all(rows, axes, 0, 0, tiled=True)  39.8 us
    all_to_all x4, waiting for transfers between devices, exchange(): return lax.all_to_all(rows, axes, 0, 0, tiled=True)  16.5 us
    all_gather x1, blocking collectives, per_device(): both = lax.all_gather(features, 'y_hi', axis=0, tiled=True)  9.76 us
    ppermute x1, starting transfers between devices, per_device(): came = lax.ppermute(send, 'y_hi', swap)  6.97 us
    ppermute x1, waiting for transfers between devices, per_device(): came = second = lax.ppermute(send, 'x', [(i, 3 - i) for i in range(4)])  6.25 us
    ppermute x1, waiting for transfers between devices, per_device(): came = lax.ppermute(send, 'y_hi', swap)  5.63 us
    ppermute x1, starting transfers between devices, per_device(): came = lax.ppermute(send, 'x', [(i, i ^ 1) for i in range(4)])  3.14 us
    ppermute x1, starting transfers between devices, per_device(): came = second = lax.ppermute(send, 'x', [(i, 3 - i) for i in range(4)])  2.83 us
  transfers between devices with their start and end apart: 7, of which 5 were waited for; matrix products, arithmetic and copies ran while one was open for 1% of the time, Pallas kernels for 1%

profile of v4, /device:TPU:1, one launch (start us, length us, event | category | flops | bytes accessed | tf_op | source)
XLA Modules:
  0.0 100.4 jit_solution(3613078225215912992)
XLA Ops:
  0.6 9.8 %all_gather.3.source = bf16[512,256]{1,0:T(8,128)(2,1)S(1)} all-gather(bf16[256,256]{1,0:T(8,128)(2,1)} %feats.1), channel_id=1, replica_groups=mesh['y_lo'=4,'z'=12,'core'=2,'y_hi'=2,'x'=4] {'y_hi'}, dimensions={0}, use_global_device_ids=true | all-gather | bytes 393216 | tf_op jit(solution)/shard_map/all_gather | solution.py:205
  10.4 1.0 %shard_map.102 = bf16[4,512,256]{2,1,0:T(8,128)(2,1)} custom-call(bf16[512,256]{1,0:T(8,128)(2,1)S(1)} %all_gather.3.source), custom_call_target="tpu_custom_call" | custom-call | tf_op jit(solution)/shard_map/pallas_call | solution.py:207
  11.4 4.9 %all-to-all-start = ((bf16[4,512,256]{2,1,0:T(8,128)(2,1)}), bf16[4,512,256]{2,1,0:T(8,128)(2,1)S(1)}, u32[]{:S(2)}, u32[]{:S(2)}) async-start(bf16[4,512,256]{2,1,0:T(8,128)(2,1)} %shard_map.102), calls=%async_computation | async-start | bytes 2097152 | tf_op jit(solution)/shard_map/all_to_all | solution.py:192
  16.3 0.7 copy-done.6
  17.1 0.1 copy.11
  17.2 0.8 copy-done.3
  18.1 0.1 copy.14.w_neigh_t
  18.2 0.1 copy.13.w_self_t
  18.4 0.6 copy-done.5
  19.1 6.9 %all-to-all-done = bf16[4,512,256]{2,1,0:T(8,128)(2,1)S(1)} async-done(((bf16[4,512,256]{2,1,0:T(8,128)(2,1)}), bf16[4,512,256]{2,1,0:T(8,128)(2,1)S(1)}, u32[]{:S(2)}, u32[]{:S(2)}) %all-to-all-start) | async-done | bytes 1048608 | tf_op jit(solution)/shard_map/all_to_all | solution.py:192
  26.0 2.3 %shard_map.103 = (bf16[768,128]{1,0:T(8,128)(2,1)}, f32[8,176,128]{2,1,0:T(8,128)S(1)}, bf16[8,176,128]{2,1,0:T(8,128)(2,1)S(1)}, f32[256,256]{1,0:T(8,128)S(1)}) custom-call(s32[16]{0:T(128)S(1)} %pad_add_fusion.table, bf16[2048,256]{1,0:T(8,128)(2,1)S(1)} %bitcast.13, bf16[256,256]{1,0:T(8,128)(2,1)S(1)} %copy-done, bf16[176,256]{1,0:T(8,128)(2,1)S(1)} %copy.13.w_self_t, ...), custom_call_target="tpu_custom_call" | custom-call | tf_op jit(solution)/shard_map/pallas_call | solution.py:211
  28.4 12.5 %all-to-all-start.1 = ((bf16[32,24,128]{2,1,0:T(8,128)(2,1)}), bf16[32,24,128]{2,1,0:T(8,128)(2,1)S(1)}, u32[]{:S(2)}, u32[]{:S(2)}) async-start(bf16[32,24,128]{2,1,0:T(8,128)(2,1)} %bitcast.6), calls=%async_computation.1 | async-start | bytes 393216 | tf_op jit(solution)/shard_map/all_to_all | solution.py:192
  40.9 3.1 %collective-permute-start = (bf16[8,176,128]{2,1,0:T(8,128)(2,1)S(1)}, bf16[8,176,128]{2,1,0:T(8,128)(2,1)S(1)}, u32[]{:S(2)}, u32[]{:S(2)}) collective-permute-start(bf16[8,176,128]{2,1,0:T(8,128)(2,1)S(1)} %get-tuple-element.18), channel_id=1, source_target_pairs={{0,1},{1,0},{2,3},{3,2},{4,5},{5,4},{6,7},{7,6},{8,9},{9,8},{10,11... | collective-permute-start | bytes 1081352 | tf_op jit(solution)/shard_map/ppermute | solution.py:226
  44.0 6.3 %all-to-all-done.1.pieces = bf16[32,24,128]{2,1,0:T(8,128)(2,1)S(1)} async-done(((bf16[32,24,128]{2,1,0:T(8,128)(2,1)}), bf16[32,24,128]{2,1,0:T(8,128)(2,1)S(1)}, u32[]{:S(2)}, u32[]{:S(2)}) %all-to-all-start.1) | async-done | bytes 196640 | tf_op jit(solution)/shard_map/all_to_all | solution.py:192
  50.3 0.7 shard_map.104
  51.0 18.6 %all-to-all-start.2 = ((bf16[24,24,128]{2,1,0:T(8,128)(2,1)}), bf16[24,24,128]{2,1,0:T(8,128)(2,1)S(1)}, u32[]{:S(2)}, u32[]{:S(2)}) async-start(bf16[24,24,128]{2,1,0:T(8,128)(2,1)} %shard_map.104), calls=%async_computation.2 | async-start | bytes 294912 | tf_op jit(solution)/shard_map/all_to_all | solution.py:192
  69.7 2.8 %collective-permute-start.1 = (bf16[4,176,128]{2,1,0:T(8,128)(2,1)S(1)}, bf16[4,176,128]{2,1,0:T(8,128)(2,1)S(1)}, u32[]{:S(2)}, u32[]{:S(2)}) collective-permute-start(bf16[4,176,128]{2,1,0:T(8,128)(2,1)S(1)} %get-tuple-element.19), channel_id=1, source_target_pairs={{0,3},{1,2},{2,1},{3,0},{4,7},{5,6},{6,5},{7,4},{8,11},{9,10},{10,... | collective-permute-start | bytes 540680 | tf_op jit(solution)/shard_map/ppermute | solution.py:228
  72.6 6.2 %collective-permute-done.1.after.came = bf16[4,176,128]{2,1,0:T(8,128)(2,1)S(1)} collective-permute-done((bf16[4,176,128]{2,1,0:T(8,128)(2,1)S(1)}, bf16[4,176,128]{2,1,0:T(8,128)(2,1)S(1)}, u32[]{:S(2)}, u32[]{:S(2)}) %collective-permute-start.1) | collective-permute-done | bytes 180256 | tf_op jit(solution)/shard_map/ppermute | solution.py:228
  78.8 3.3 %all-to-all-done.2.pieces = bf16[24,24,128]{2,1,0:T(8,128)(2,1)S(1)} async-done(((bf16[24,24,128]{2,1,0:T(8,128)(2,1)}), bf16[24,24,128]{2,1,0:T(8,128)(2,1)S(1)}, u32[]{:S(2)}, u32[]{:S(2)}) %all-to-all-start.2) | async-done | bytes 147488 | tf_op jit(solution)/shard_map/all_to_all | solution.py:192
  82.1 0.7 shard_map.106
  82.8 3.9 %all-to-all-start.3 = ((bf16[32,24,128]{2,1,0:T(8,128)(2,1)}), bf16[32,24,128]{2,1,0:T(8,128)(2,1)S(1)}, u32[]{:S(2)}, u32[]{:S(2)}) async-start(bf16[32,24,128]{2,1,0:T(8,128)(2,1)} %shard_map.106), calls=%async_computation.3 | async-start | bytes 393216 | tf_op jit(solution)/shard_map/all_to_all | solution.py:192
  86.7 7.0 %collective-permute-start.2 = (bf16[2,176,128]{2,1,0:T(8,128)(2,1)S(1)}, bf16[2,176,128]{2,1,0:T(8,128)(2,1)S(1)}, u32[]{:S(2)}, u32[]{:S(2)}) collective-permute-start(bf16[2,176,128]{2,1,0:T(8,128)(2,1)S(1)} %get-tuple-element.22), channel_id=1, source_target_pairs={{0,4},{4,0},{1,5},{5,1},{2,6},{6,2},{3,7},{7,3},{8,12},{12,8},{9,1... | collective-permute-start | bytes 270344 | tf_op jit(solution)/shard_map/ppermute | solution.py:230
  93.7 5.6 %collective-permute-done.2.came = bf16[2,176,128]{2,1,0:T(8,128)(2,1)S(1)} collective-permute-done((bf16[2,176,128]{2,1,0:T(8,128)(2,1)S(1)}, bf16[2,176,128]{2,1,0:T(8,128)(2,1)S(1)}, u32[]{:S(2)}, u32[]{:S(2)}) %collective-permute-start.2) | collective-permute-done | bytes 90144 | tf_op jit(solution)/shard_map/ppermute | solution.py:230
  99.3 1.0 %shard_map.108 = (f32[1,1]{1,0:T(1,128)}, f32[172,256]{1,0:T(8,128)}, f32[172,256]{1,0:T(8,128)}, bf16[256,256]{1,0:T(8,128)(2,1)}) custom-call(bf16[768,128]{1,0:T(8,128)(2,1)S(1)} %bitcast.14, f32[2,176,128]{2,1,0:T(8,128)S(1)} %get-tuple-element.21.kept, bf16[2,176,128]{2,1,0:T(8,128)(2,1)S(1)} %collective-permute-done.2.came, ...), custom_call_target="tpu_custom_call" | custom-call | tf_op jit(solution)/shard_map/pallas_call | solution.py:236
  (21 shorter events, 0.4 us)
Async XLA Ops:
  11.4 5.6 %copy-start.2 = (bf16[256,172]{0,1:T(8,128)(2,1)S(1)}, bf16[256,172]{0,1:T(8,128)(2,1)}, u32[]{:S(2)}) copy-start(bf16[256,172]{0,1:T(8,128)(2,1)} %param.8) | copy-start | bytes 264196
  11.4 14.6 %all-to-all-start = ((bf16[4,512,256]{2,1,0:T(8,128)(2,1)}), bf16[4,512,256]{2,1,0:T(8,128)(2,1)S(1)}, u32[]{:S(2)}, u32[]{:S(2)}) async-start(bf16[4,512,256]{2,1,0:T(8,128)(2,1)} %shard_map.102), calls=%async_computation | async-start | bytes 2097152 | tf_op jit(solution)/shard_map/all_to_all | solution.py:192
  16.3 0.7 copy-start.6
  17.1 0.9 copy-start.3
  18.1 8.0 %copy-start.1 = (bf16[2,6,128,128]{3,2,1,0:T(8,128)(2,1)S(1)}, bf16[2,6,128,128]{3,2,1,0:T(8,128)(2,1)}, u32[]{:S(2)}) copy-start(bf16[2,6,128,128]{3,2,1,0:T(8,128)(2,1)} %values.1) | copy-start | bytes 1179652
  18.2 7.8 %copy-start = (bf16[256,256]{1,0:T(8,128)(2,1)S(1)}, bf16[256,256]{1,0:T(8,128)(2,1)}, u32[]{:S(2)}) copy-start(bf16[256,256]{1,0:T(8,128)(2,1)} %feats.1) | copy-start | bytes 393220
  18.4 0.7 copy-start.5
  19.0 7.0 %copy-start.4 = (s32[256]{0:T(256)S(1)}, s32[256]{0:T(256)}, u32[]{:S(2)}) copy-start(s32[256]{0:T(256)} %param.13) | copy-start | bytes 3076
  28.4 22.0 %all-to-all-start.1 = ((bf16[32,24,128]{2,1,0:T(8,128)(2,1)}), bf16[32,24,128]{2,1,0:T(8,128)(2,1)S(1)}, u32[]{:S(2)}, u32[]{:S(2)}) async-start(bf16[32,24,128]{2,1,0:T(8,128)(2,1)} %bitcast.6), calls=%async_computation.1 | async-start | bytes 393216 | tf_op jit(solution)/shard_map/all_to_all | solution.py:192
  40.9 28.8 %collective-permute-start = (bf16[8,176,128]{2,1,0:T(8,128)(2,1)S(1)}, bf16[8,176,128]{2,1,0:T(8,128)(2,1)S(1)}, u32[]{:S(2)}, u32[]{:S(2)}) collective-permute-start(bf16[8,176,128]{2,1,0:T(8,128)(2,1)S(1)} %get-tuple-element.18), channel_id=1, source_target_pairs={{0,1},{1,0},{2,3},{3,2},{4,5},{5,4},{6,7},{7,6},{8,9},{9,8},{10,11... | collective-permute-start | bytes 1081352 | tf_op jit(solution)/shard_map/ppermute | solution.py:226
  51.0 31.1 %all-to-all-start.2 = ((bf16[24,24,128]{2,1,0:T(8,128)(2,1)}), bf16[24,24,128]{2,1,0:T(8,128)(2,1)S(1)}, u32[]{:S(2)}, u32[]{:S(2)}) async-start(bf16[24,24,128]{2,1,0:T(8,128)(2,1)} %shard_map.104), calls=%async_computation.2 | async-start | bytes 294912 | tf_op jit(solution)/shard_map/all_to_all | solution.py:192
  69.7 9.1 %collective-permute-start.1 = (bf16[4,176,128]{2,1,0:T(8,128)(2,1)S(1)}, bf16[4,176,128]{2,1,0:T(8,128)(2,1)S(1)}, u32[]{:S(2)}, u32[]{:S(2)}) collective-permute-start(bf16[4,176,128]{2,1,0:T(8,128)(2,1)S(1)} %get-tuple-element.19), channel_id=1, source_target_pairs={{0,3},{1,2},{2,1},{3,0},{4,7},{5,6},{6,5},{7,4},{8,11},{9,10},{10,... | collective-permute-start | bytes 540680 | tf_op jit(solution)/shard_map/ppermute | solution.py:228
  82.8 16.5 %all-to-all-start.3 = ((bf16[32,24,128]{2,1,0:T(8,128)(2,1)}), bf16[32,24,128]{2,1,0:T(8,128)(2,1)S(1)}, u32[]{:S(2)}, u32[]{:S(2)}) async-start(bf16[32,24,128]{2,1,0:T(8,128)(2,1)} %shard_map.106), calls=%async_computation.3 | async-start | bytes 393216 | tf_op jit(solution)/shard_map/all_to_all | solution.py:192
  86.7 12.6 %collective-permute-start.2 = (bf16[2,176,128]{2,1,0:T(8,128)(2,1)S(1)}, bf16[2,176,128]{2,1,0:T(8,128)(2,1)S(1)}, u32[]{:S(2)}, u32[]{:S(2)}) collective-permute-start(bf16[2,176,128]{2,1,0:T(8,128)(2,1)S(1)} %get-tuple-element.22), channel_id=1, source_target_pairs={{0,4},{4,0},{1,5},{5,1},{2,6},{6,2},{3,7},{7,3},{8,12},{12,8},{9,1... | collective-permute-start | bytes 270344 | tf_op jit(solution)/shard_map/ppermute | solution.py:230
